TPU v7x, 32 devices: a whole 2x2x4 slice. The times are simulated.
32 devices in a mesh: grp: 2 (over x), aa: 16 (over z, y, core).
Axes of the slice: x: 2, y: 2, z: 4, core: 2. Of those that a mesh axis runs over, the one named last changes fastest.
Arguments:
- amplitudes: float32 [96, 128, 128], P('aa', 'grp'), parts along dimension 1, may hold values from -6 to 6
- integrals: float32 [6144, 16, 128], P(('grp', 'aa')), parts along dimension 0, may hold values from -0.125 to 0.125
- irrep_sizes: int32 [8], replicated, may hold values from 1 to 16, 96 in all
- home: int32 [96], replicated, may hold values from 0 to 95, as said below
- row_irrep: int32 [16], replicated, may hold values from 0 to 7
Outputs:
- residual: float32 [128, 3072], P('grp', 'aa'), parts along dimension 0
There are 2 independent parts, one for each index of `grp`. A program takes and returns all parts, laid end to end along the dimension named above; an argument that names none is the same for every part. Nothing has to cross between parts.
Inputs may be any that keep to these rules, and one draw needn't show every extreme that they name: `home`: a permutation of 0 .. 95; the positions of one irrep map to rows on distinct indices of aa (row // 6).
All inputs are finite; a program needn't handle non-finite values.
Results may differ from a plain program's by a relative error of at most 0.0003.
Values sent between devices are 32-bit elements; how exact they have to be, the bound alone decides.
A program may use at most 192 MiB of HBM per device.

v0:
```python
import jax
import jax.numpy as jnp
from jax import lax
from jax.sharding import PartitionSpec as P


def body(amplitudes, integrals, irrep_sizes, home, row_irrep):
    most = integrals.shape[1]
    total = home.shape[0]
    irreps = irrep_sizes.shape[0]
    myself = lax.axis_index("aa")
    offsets = jnp.cumsum(irrep_sizes) - irrep_sizes
    labels = jnp.arange(irreps, dtype=jnp.int32)
    my_irrep = row_irrep[myself]
    start_pos = jnp.sum(jnp.where(labels == my_irrep, offsets, 0))
    count = jnp.sum(jnp.where(labels == my_irrep, irrep_sizes, 0))
    slots = jnp.arange(most, dtype=jnp.int32)
    positions = jnp.clip(start_pos + slots, 0, total - 1)
    store_rows = home[positions]
    alive = slots < count
    shard_rows = lax.all_gather(amplitudes, "aa", axis=0, tiled=True)
    width = shard_rows.shape[0]
    chooser = (store_rows[:, None] == jnp.arange(width, dtype=jnp.int32)[None, :]) & alive[:, None]
    selected = jnp.einsum(
        "mq,qpc->mpc", chooser.astype(jnp.float32), shard_rows, precision=lax.Precision.HIGHEST
    )
    return 0.5 * jnp.einsum("mpc,rmc->pr", selected, integrals, precision=lax.Precision.HIGHEST)


def solution(mesh):
    return jax.shard_map(
        body,
        mesh=mesh,
        in_specs=(P("aa", "grp", None), P(("grp", "aa"), None, None), P(), P(), P()),
        out_specs=P("grp", "aa"),
        check_vma=False,
    )
```

profile of v0, /device:TPU:0, one launch (start us, length us, event | category | flops | bytes accessed | tf_op | source)
XLA Modules:
  0.0 71.6 jit_solution(52677280663145075)
XLA Ops:
  6.5 0.0 copy-start
  6.5 0.0 all-gather.2.cloned.1.call-start
  6.5 0.7 all-gather.2.cloned.1.call-update
  7.3 0.8 %reduce-window.9 = s32[8,1]{0,1:T(1,128)S(1)} reduce-window(s32[8,1]{0,1:T(1,128)} %bitcast.15, s32[]{:T(128)} %constant.6.clone.1), window={size=8x1 pad=7_0x0_0}, to_apply=%region_0.0 | reduce-window | flops 56 | bytes 68 | tf_op jit(solution)/shard_map/reduce-window.4
  8.1 1.2 %dynamic_slice.3 = s32[1]{0:T(128)} dynamic-slice(s32[16]{0:T(128)} %param.9, s32[]{:T(128)S(6)} %select_n.20), dynamic_slice_sizes={1} | dynamic-slice | bytes 12 | tf_op jit(solution)/shard_map/dynamic_slice | solution.py:14
  9.3 2.0 %fusion.17 = (s32[]{:T(128)}, s32[]{:T(128)}) fusion(s32[8]{0:T(128)} %param.7, s32[]{:T(128)} %bitcast, s32[8,1]{0,1:T(1,128)S(1)} %reduce-window.9), kind=kLoop, calls=%fused_computation.18 | loop fusion | flops 46 | bytes 76 | tf_op jit(solution)/shard_map/reduce_sum | solution.py:16
  11.3 0.6 fusion.18
  11.9 1.3 %gather_fusion = s32[16]{0:T(128)S(1)} fusion(s32[96]{0:T(128)} %param.8, s32[1024]{0:T(1024)S(1)} %pad_clamp_fusion), kind=kCustom, calls=%fused_computation | custom fusion | bytes 192 | tf_op jit(solution)/shard_map/gather | solution.py:19
  13.2 0.6 iota_compare_fusion.1
  13.8 43.8 %all-gather.2.cloned.1.call-done = f32[96,64,128]{2,1,0:T(8,128)} async-done(((f32[6,64,128]{2,1,0:T(8,128)}), f32[96,64,128]{2,1,0:T(8,128)}) %all-gather.2.cloned.1.call-update) | async-done | bytes 3145744 | tf_op jit(solution)/shard_map/all_gather | solution.py:21
  57.6 4.6 %fusion = f32[16,64,128]{2,0,1:T(8,128)S(1)} fusion(f32[96,64,128]{2,1,0:T(8,128)} %all-gather.2.cloned.1.call-done, s32[16]{0:T(128)S(1)} %gather_fusion, pred[16]{0:T(512)(128)(4,1)S(1)} %iota_compare_fusion.1), kind=kOutput, calls=%fused_computation.1 | convolution fusion | flops 150998016 | bytes 3670096 | tf_op jit(solution)/shard_map/mq,qpc->mpc/dot_general | solution.py:24
  62.2 0.0 copy-done
  62.2 2.5 %fusion.7 = f32[64,192]{1,0:T(8,128)} fusion(f32[192,16,128]{2,1,0:T(8,128)S(1)} %copy-done, f32[16,64,128]{2,0,1:T(8,128)S(1)} %fusion), kind=kOutput, calls=%fused_computation.6 | convolution fusion | flops 302002176 | bytes 2146304 | tf_op jit(solution)/shard_map/mpc,rmc->pr/dot_general | solution.py:27
  (1 shorter events, 0.0 us)
Async XLA Ops:
  6.5 55.7 %copy-start = (f32[192,16,128]{2,1,0:T(8,128)S(1)}, f32[192,16,128]{2,1,0:T(8,128)}, u32[]{:S(2)}) copy-start(f32[192,16,128]{2,1,0:T(8,128)} %param.6) | copy-start | bytes 4718596
  6.5 51.0 %all-gather.2.cloned.1.call-start = ((), (), s32[]{:S(2)}) async-start(), calls=%async_computation | async-start | bytes 3342336 | tf_op jit(solution)/shard_map/all_gather | solution.py:21
Sparse Core Ops, SparseCore 0:
  9.6 47.8 all-gather.1
where the time goes:
time: 71.8 us; the launch traced here: 71.6 us
  waiting for transfers between devices  44.5 us (62%)
  between operations  13.4 us (19%)
  matrix products  7.15 us (10%)
  other arithmetic  3.97 us (6%)
  local copies, waits for them, and re-layouts  2.56 us (4%)
    all_gather x1, waiting for transfers between devices, body(): shard_rows = lax.all_gather(amplitudes, 'aa', axis=0, tiled=True)  43.8 us
    dot_general x1, matrix products, body(): jnp.einsum('mq,qpc->mpc', chooser.astype(jnp.float32), shard_rows, precis...  4.62 us
    dot_general x1, matrix products, body(): jnp.einsum('mpc,rmc->pr', selected, integrals, precision=lax.Precision.HI...  2.53 us
    reduce_sum x1, other arithmetic, body(): count = jnp.sum(jnp.where(labels == my_irrep, irrep_sizes, 0))  1.95 us
  transfers between devices with their start and end apart: 1, of which 1 were waited for; matrix products, arithmetic and copies ran while one was open for 9% of the time, Pallas kernels for 0%

commit v1 on v0

v1 whole, which is shorter than its diff:
```python
import functools

import jax
import jax.numpy as jnp
from jax import lax
from jax.experimental import pallas as pl
from jax.experimental.pallas import tpu as pltpu
from jax.sharding import PartitionSpec as P

MESH = pl.DeviceIdType.MESH
UNROLL = 16


def each(first, last, step):
    if last - first <= UNROLL:
        for i in range(first, last):
            step(i)
    else:
        lax.fori_loop(first, last, lambda i, _: (step(i), 0)[1], 0)


def flipped(me, k, n):
    out, bit = me, 1
    while bit < n:
        mine = lax.rem(lax.div(me, bit), 2)
        flip = (k // bit) % 2
        out = out + flip * bit * (1 - 2 * mine)
        bit *= 2
    return out


def scan(count, step, init):
    chunk = 8 if count % 8 == 0 else 1

    def some(outer, state):
        for inner in range(chunk):
            state = step(outer * chunk + inner, state)
        return state

    return lax.fori_loop(0, count // chunk, some, init)


def kernel(n, most, sizes, home, row_irrep, amp, integ, out,
           amp_v, integ_v, send, recv, high, low, slot_of,
           amp_sem, integ_sem, send_sem, recv_sem):
    me = lax.axis_index("aa")
    per = amp.shape[0]
    irreps, total = sizes.shape[0], home.shape[0]
    rows = high.shape[1]

    barrier = pltpu.get_barrier_semaphore()
    each(1, n, lambda k: pl.semaphore_signal(
        barrier, inc=1, device_id={"aa": flipped(me, k, n)}, device_id_type=MESH))
    get_amp = pltpu.make_async_copy(amp, amp_v, amp_sem)
    get_amp.start()
    get_integ = pltpu.make_async_copy(integ, integ_v, integ_sem)
    get_integ.start()

    offsets, at = [], jnp.int32(0)
    for g in range(irreps):
        offsets.append(at)
        at = at + sizes[g]

    def look(i, found):
        which = home[i] - me * per
        return tuple(jnp.where(which == q, i, found[q]) for q in range(per))

    places = scan(total, look, tuple(jnp.int32(0) for _ in range(per)))
    kinds = [sum((p >= offsets[g]).astype(jnp.int32) for g in range(1, irreps)) for p in places]

    get_amp.wait()

    def stage(k):
        dest = flipped(me, k, n)
        wanted = row_irrep[dest]
        pick = jnp.int32(0)
        has = jnp.bool_(False)
        for q in range(per):
            pick = jnp.where(kinds[q] == wanted, q, pick)
            has = has | (kinds[q] == wanted)
        block = amp_v[pick]
        send[dest] = jnp.where(has, block, 0.0)

    each(0, n, stage)

    def hop(k):
        peer = flipped(me, k, n)
        return pltpu.make_async_remote_copy(
            src_ref=send.at[peer], dst_ref=recv.at[me],
            send_sem=send_sem.at[peer], recv_sem=recv_sem.at[me],
            device_id={"aa": peer}, device_id_type=MESH)

    def landing(peer):
        return pltpu.make_async_remote_copy(
            src_ref=send.at[peer], dst_ref=recv.at[peer],
            send_sem=send_sem.at[peer], recv_sem=recv_sem.at[peer],
            device_id={"aa": peer}, device_id_type=MESH)

    pl.semaphore_wait(barrier, n - 1)
    each(0, n - 1, lambda i: hop(n - 1 - i).start())

    mine = row_irrep[me]
    start = jnp.int32(0)
    count = jnp.int32(0)
    for g in range(irreps):
        start = jnp.where(mine == g, offsets[g], start)
        count = jnp.where(mine == g, sizes[g], count)

    def find(source):
        def look_at(m, found):
            row = home[jnp.minimum(start + m, total - 1)] - source * per
            return jnp.where((row >= 0) & (row < per) & (m < count), m, found)

        slot_of[source] = scan(most, look_at, jnp.int32(0))

    each(0, n, find)

    get_integ.wait()

    def split(m):
        full = integ_v[pl.ds(m, rows, stride=most), :]
        top = full.astype(jnp.bfloat16)
        high[m] = top
        low[m] = (full - top.astype(jnp.float32)).astype(jnp.bfloat16)

    each(0, most, split)

    contract = (((1,), (1,)), ((), ()))

    def times(blocks, sources):
        full = jnp.concatenate(blocks, axis=1)
        top = full.astype(jnp.bfloat16)
        rest = (full - top.astype(jnp.float32)).astype(jnp.bfloat16)
        slots = [slot_of[s] for s in sources]
        upper = jnp.concatenate([high[m] for m in slots], axis=1)
        lower = jnp.concatenate([low[m] for m in slots], axis=1)
        both = lax.dot_general(jnp.concatenate([top, rest], axis=0), upper, contract,
                               preferred_element_type=jnp.float32)
        small = lax.dot_general(top, lower, contract, preferred_element_type=jnp.float32)
        half = top.shape[0]
        return both[:half] + (both[half:] + small)

    twin = flipped(me, 1, n)
    landing(twin).wait_recv()
    out[...] = times([send[me], recv[twin]], [me, twin])

    def pair(i):
        one, two = flipped(me, 2 * i, n), flipped(me, 2 * i + 1, n)
        landing(one).wait_recv()
        landing(two).wait_recv()
        out[...] += times([recv[one], recv[two]], [one, two])

    each(1, n // 2, pair)
    out[...] = 0.5 * out[...]
    each(1, n, lambda k: hop(k).wait_send())


def solution(mesh):
    n = mesh.shape["aa"]

    def body(amplitudes, integrals, irrep_sizes, home, row_irrep):
        per, pairs, width = amplitudes.shape
        rows, most, _ = integrals.shape
        smem = pl.BlockSpec(memory_space=pltpu.SMEM)
        hbm = pl.BlockSpec(memory_space=pl.ANY)
        return pl.pallas_call(
            functools.partial(kernel, n, most),
            out_shape=jax.ShapeDtypeStruct((pairs, rows), jnp.float32),
            in_specs=[smem, smem, smem, hbm, hbm],
            out_specs=pl.BlockSpec(memory_space=pltpu.VMEM),
            scratch_shapes=[
                pltpu.VMEM((per, pairs, width), jnp.float32),
                pltpu.VMEM((rows * most, width), jnp.float32),
                pltpu.VMEM((n, pairs, width), jnp.float32),
                pltpu.VMEM((n, pairs, width), jnp.float32),
                pltpu.VMEM((most, rows, width), jnp.bfloat16),
                pltpu.VMEM((most, rows, width), jnp.bfloat16),
                pltpu.SMEM((n,), jnp.int32),
                pltpu.SemaphoreType.DMA,
                pltpu.SemaphoreType.DMA,
                pltpu.SemaphoreType.DMA((n,)),
                pltpu.SemaphoreType.DMA((n,)),
            ],
            compiler_params=pltpu.CompilerParams(
                collective_id=0, has_side_effects=True, vmem_limit_bytes=56 << 20),
        )(irrep_sizes, home, row_irrep, amplitudes, integrals.reshape(rows * most, width))

    return jax.shard_map(
        body,
        mesh=mesh,
        in_specs=(P("aa", "grp", None), P(("grp", "aa"), None, None), P(), P(), P()),
        out_specs=P("grp", "aa"),
        check_vma=False,
    )
```

time: 71.8 us -> 23.1 us (0.32)
  waiting for transfers between devices: 44.5 us -> 0 us
  Pallas kernels: 0 us -> 21.4 us
  between operations: 13.4 us -> 0.01 us
  matrix products: 7.15 us -> 0 us
  other arithmetic: 3.97 us -> 0 us
  local copies, waits for them, and re-layouts: 2.56 us -> 1.47 us
    all_gather x1 -> x0, waiting for transfers between devices: 43.8 us -> none  [body(): shard_rows = lax.all_gather(amplitudes, 'aa', axis=0, tiled=True)]
    pallas_call x0 -> x1, Pallas kernels: none -> 21.4 us  [body(): pl.pallas_call(functools.partial(kernel, n, most), out_shape=jax.ShapeDty...]
    dot_general x2 -> x0, matrix products: 7.15 us -> none  [the longest x1 4.62 us: body(): jnp.einsum('mq,qpc->mpc', chooser.astype(jnp.float32), shard_rows, precis...]
    reduce_sum x1 -> x0, other arithmetic: 1.95 us -> none  [body(): count = jnp.sum(jnp.where(labels == my_irrep, irrep_sizes, 0))]
    unnamed x2 -> x1, local copies, waits for them, and re-layouts: 0.01 us -> 1.47 us
    gather x1 -> x0, local copies, waits for them, and re-layouts: 1.32 us -> none  [body(): store_rows = home[positions]]
    dynamic_slice x1 -> x0, local copies, waits for them, and re-layouts: 1.24 us -> none  [body(): my_irrep = row_irrep[myself]]
    another operation x1 -> x0, other arithmetic: 0.83 us -> none
  transfers between devices with their start and end apart: 1 -> 0, of which waited for: 1 -> 0; matrix products, arithmetic and copies ran while one was open for 9% -> 0% of each run, Pallas kernels for 0% -> 0%
where the time goes in v1:
time: 23.1 us; the launch traced here: 22.9 us
  Pallas kernels  21.4 us (93%)
  local copies, waits for them, and re-layouts  1.47 us (6%)
    pallas_call x1, Pallas kernels, body(): pl.pallas_call(functools.partial(kernel, n, most), out_shape=jax.ShapeDty...  21.4 us
    unnamed x1, local copies, waits for them, and re-layouts  1.47 us

profile of v1, /device:TPU:0, one launch (start us, length us, event | category | flops | bytes accessed | tf_op | source)
XLA Modules:
  0.0 22.9 jit_solution(336801849497893772)
XLA Ops:
  0.0 21.4 %shard_map.55 = f32[64,192]{1,0:T(8,128)} custom-call(s32[8]{0:T(128)} %sizes.1, s32[96]{0:T(128)} %home.1, s32[16]{0:T(128)} %row_irrep.1, f32[6,64,128]{2,1,0:T(8,128)} %amp.1, f32[3072,128]{1,0:T(8,128)} %bitcast.1), custom_call_target="tpu_custom_call" | custom-call | tf_op jit(solution)/shard_map/pallas_call | solution.py:166
  21.4 1.5 %copy.7 = f32[64,192]{1,0:T(8,128)} copy(f32[64,192]{1,0:T(8,128)} %shard_map.55) | data formatting | bytes 98304

commit v2 on v1

--- a/solution.py
+++ b/solution.py
@@ -40,9 +40,10 @@
     return lax.fori_loop(0, count // chunk, some, init)
 
 
-def kernel(n, most, sizes, home, row_irrep, amp, integ, out,
+def kernel(n, most, sizes_in, home_in, row_irrep_in, amp, integ, out,
+           sizes, home, row_irrep,
            amp_v, integ_v, send, recv, high, low, slot_of,
-           amp_sem, integ_sem, send_sem, recv_sem):
+           index_sem, amp_sem, integ_sem, send_sem, recv_sem):
     me = lax.axis_index("aa")
     per = amp.shape[0]
     irreps, total = sizes.shape[0], home.shape[0]
@@ -51,11 +52,17 @@
     barrier = pltpu.get_barrier_semaphore()
     each(1, n, lambda k: pl.semaphore_signal(
         barrier, inc=1, device_id={"aa": flipped(me, k, n)}, device_id_type=MESH))
+    get_index = [pltpu.make_async_copy(source, dest, index_sem.at[i]) for i, (source, dest) in enumerate(
+        ((home_in, home), (sizes_in, sizes), (row_irrep_in, row_irrep)))]
+    for copy in get_index:
+        copy.start()
     get_amp = pltpu.make_async_copy(amp, amp_v, amp_sem)
     get_amp.start()
     get_integ = pltpu.make_async_copy(integ, integ_v, integ_sem)
     get_integ.start()
 
+    for copy in get_index:
+        copy.wait()
     offsets, at = [], jnp.int32(0)
     for g in range(irreps):
         offsets.append(at)
@@ -97,7 +104,7 @@
             device_id={"aa": peer}, device_id_type=MESH)
 
     pl.semaphore_wait(barrier, n - 1)
-    each(0, n - 1, lambda i: hop(n - 1 - i).start())
+    each(0, n - 1, lambda i: hop(i + 1).start())
 
     mine = row_irrep[me]
     start = jnp.int32(0)
@@ -161,14 +168,16 @@
     def body(amplitudes, integrals, irrep_sizes, home, row_irrep):
         per, pairs, width = amplitudes.shape
         rows, most, _ = integrals.shape
-        smem = pl.BlockSpec(memory_space=pltpu.SMEM)
-        hbm = pl.BlockSpec(memory_space=pl.ANY)
+        hbm = pl.BlockSpec(memory_space=pltpu.HBM)
         return pl.pallas_call(
             functools.partial(kernel, n, most),
-            out_shape=jax.ShapeDtypeStruct((pairs, rows), jnp.float32),
-            in_specs=[smem, smem, smem, hbm, hbm],
+            out_shape=pltpu.VMEM((pairs, rows), jnp.float32),
+            in_specs=[hbm] * 5,
             out_specs=pl.BlockSpec(memory_space=pltpu.VMEM),
             scratch_shapes=[
+                pltpu.SMEM(irrep_sizes.shape, jnp.int32),
+                pltpu.SMEM(home.shape, jnp.int32),
+                pltpu.SMEM(row_irrep.shape, jnp.int32),
                 pltpu.VMEM((per, pairs, width), jnp.float32),
                 pltpu.VMEM((rows * most, width), jnp.float32),
                 pltpu.VMEM((n, pairs, width), jnp.float32),
@@ -176,6 +185,7 @@
                 pltpu.VMEM((most, rows, width), jnp.bfloat16),
                 pltpu.VMEM((most, rows, width), jnp.bfloat16),
                 pltpu.SMEM((n,), jnp.int32),
+                pltpu.SemaphoreType.DMA((3,)),
                 pltpu.SemaphoreType.DMA,
                 pltpu.SemaphoreType.DMA,
                 pltpu.SemaphoreType.DMA((n,)),

time: 23.1 us -> 17.8 us (0.77)
  Pallas kernels: 21.4 us -> 17 us
  local copies, waits for them, and re-layouts: 1.47 us -> 0.63 us
    pallas_call x1, Pallas kernels: 21.4 us -> 17 us  [body(): pl.pallas_call(functools.partial(kernel, n, most), out_shape=pltpu.VMEM((...]
    unnamed x1, local copies, waits for them, and re-layouts: 1.47 us -> 0.63 us
where the time goes in v2:
time: 17.8 us; the launch traced here: 17.7 us
  Pallas kernels  17 us (96%)
  local copies, waits for them, and re-layouts  0.63 us (4%)
    pallas_call x1, Pallas kernels, body(): pl.pallas_call(functools.partial(kernel, n, most), out_shape=pltpu.VMEM((...  17 us
    unnamed x1, local copies, waits for them, and re-layouts  0.63 us

profile of v2, /device:TPU:0, one launch (start us, length us, event | category | flops | bytes accessed | tf_op | source)
XLA Modules:
  0.0 17.7 jit_solution(6873011891011247237)
XLA Ops:
  0.0 17.0 %shard_map.55 = f32[64,192]{1,0:T(8,128)S(1)} custom-call(s32[8]{0:T(128)} %sizes_in.1, s32[96]{0:T(128)} %home_in.1, s32[16]{0:T(128)} %row_irrep_in.1, f32[6,64,128]{2,1,0:T(8,128)} %amp.1, f32[3072,128]{1,0:T(8,128)} %bitcast.1), custom_call_target="tpu_custom_call" | custom-call | tf_op jit(solution)/shard_map/pallas_call | solution.py:172
  17.0 0.6 %copy.7 = f32[64,192]{1,0:T(8,128)} copy(f32[64,192]{1,0:T(8,128)S(1)} %shard_map.55) | data formatting | bytes 98304

commit v3 on v2

--- a/solution.py
+++ b/solution.py
@@ -125,7 +125,7 @@
     get_integ.wait()
 
     def split(m):
-        full = integ_v[pl.ds(m, rows, stride=most), :]
+        full = integ_v[:, m, :]
         top = full.astype(jnp.bfloat16)
         high[m] = top
         low[m] = (full - top.astype(jnp.float32)).astype(jnp.bfloat16)
@@ -157,8 +157,11 @@
         landing(two).wait_recv()
         out[...] += times([recv[one], recv[two]], [one, two])
 
-    each(1, n // 2, pair)
-    out[...] = 0.5 * out[...]
+    each(1, n // 2 - 1, pair)
+    one, two = flipped(me, n - 2, n), flipped(me, n - 1, n)
+    landing(one).wait_recv()
+    landing(two).wait_recv()
+    out[...] = 0.5 * (out[...] + times([recv[one], recv[two]], [one, two]))
     each(1, n, lambda k: hop(k).wait_send())
 
 
@@ -179,7 +182,7 @@
                 pltpu.SMEM(home.shape, jnp.int32),
                 pltpu.SMEM(row_irrep.shape, jnp.int32),
                 pltpu.VMEM((per, pairs, width), jnp.float32),
-                pltpu.VMEM((rows * most, width), jnp.float32),
+                pltpu.VMEM(integrals.shape, jnp.float32),
                 pltpu.VMEM((n, pairs, width), jnp.float32),
                 pltpu.VMEM((n, pairs, width), jnp.float32),
                 pltpu.VMEM((most, rows, width), jnp.bfloat16),
@@ -193,7 +196,7 @@
             ],
             compiler_params=pltpu.CompilerParams(
                 collective_id=0, has_side_effects=True, vmem_limit_bytes=56 << 20),
-        )(irrep_sizes, home, row_irrep, amplitudes, integrals.reshape(rows * most, width))
+        )(irrep_sizes, home, row_irrep, amplitudes, integrals)
 
     return jax.shard_map(
         body,

time: 17.8 us -> 17.8 us (level)
  no operation moved by 1% of the time
where the time goes in v3:
time: 17.8 us; the launch traced here: 17.6 us
  Pallas kernels  17 us (96%)
  local copies, waits for them, and re-layouts  0.63 us (4%)
    pallas_call x1, Pallas kernels, body(): pl.pallas_call(functools.partial(kernel, n, most), out_shape=pltpu.VMEM((...  17 us
    unnamed x1, local copies, waits for them, and re-layouts  0.63 us

profile of v3, /device:TPU:0, one launch (start us, length us, event | category | flops | bytes accessed | tf_op | source)
XLA Modules:
  0.0 17.6 jit_solution(17986442109116631611)
XLA Ops:
  0.0 17.0 %shard_map.55 = f32[64,192]{1,0:T(8,128)S(1)} custom-call(s32[8]{0:T(128)} %sizes_in.1, s32[96]{0:T(128)} %home_in.1, s32[16]{0:T(128)} %row_irrep_in.1, f32[6,64,128]{2,1,0:T(8,128)} %amp.1, f32[192,16,128]{2,1,0:T(8,128)} %integ.1), custom_call_target="tpu_custom_call" | custom-call | tf_op jit(solution)/shard_map/pallas_call | solution.py:175
  17.0 0.6 %copy.7 = f32[64,192]{1,0:T(8,128)} copy(f32[64,192]{1,0:T(8,128)S(1)} %shard_map.55) | data formatting | bytes 98304

commit v4 on v3

--- a/solution.py
+++ b/solution.py
@@ -47,7 +47,6 @@
     me = lax.axis_index("aa")
     per = amp.shape[0]
     irreps, total = sizes.shape[0], home.shape[0]
-    rows = high.shape[1]
 
     barrier = pltpu.get_barrier_semaphore()
     each(1, n, lambda k: pl.semaphore_signal(
@@ -125,22 +124,22 @@
     get_integ.wait()
 
     def split(m):
-        full = integ_v[:, m, :]
+        full = integ_v[:, m, :].T
         top = full.astype(jnp.bfloat16)
         high[m] = top
         low[m] = (full - top.astype(jnp.float32)).astype(jnp.bfloat16)
 
     each(0, most, split)
 
-    contract = (((1,), (1,)), ((), ()))
+    contract = (((1,), (0,)), ((), ()))
 
     def times(blocks, sources):
         full = jnp.concatenate(blocks, axis=1)
         top = full.astype(jnp.bfloat16)
         rest = (full - top.astype(jnp.float32)).astype(jnp.bfloat16)
         slots = [slot_of[s] for s in sources]
-        upper = jnp.concatenate([high[m] for m in slots], axis=1)
-        lower = jnp.concatenate([low[m] for m in slots], axis=1)
+        upper = jnp.concatenate([high[m] for m in slots], axis=0)
+        lower = jnp.concatenate([low[m] for m in slots], axis=0)
         both = lax.dot_general(jnp.concatenate([top, rest], axis=0), upper, contract,
                                preferred_element_type=jnp.float32)
         small = lax.dot_general(top, lower, contract, preferred_element_type=jnp.float32)
@@ -185,8 +184,8 @@
                 pltpu.VMEM(integrals.shape, jnp.float32),
                 pltpu.VMEM((n, pairs, width), jnp.float32),
                 pltpu.VMEM((n, pairs, width), jnp.float32),
-                pltpu.VMEM((most, rows, width), jnp.bfloat16),
-                pltpu.VMEM((most, rows, width), jnp.bfloat16),
+                pltpu.VMEM((most, width, rows), jnp.bfloat16),
+                pltpu.VMEM((most, width, rows), jnp.bfloat16),
                 pltpu.SMEM((n,), jnp.int32),
                 pltpu.SemaphoreType.DMA((3,)),
                 pltpu.SemaphoreType.DMA,

time: 17.8 us -> 17.8 us (level)
  no operation moved by 1% of the time
where the time goes in v4:
time: 17.8 us; the launch traced here: 17.6 us
  Pallas kernels  17 us (96%)
  local copies, waits for them, and re-layouts  0.63 us (4%)
    pallas_call x1, Pallas kernels, body(): pl.pallas_call(functools.partial(kernel, n, most), out_shape=pltpu.VMEM((...  17 us
    unnamed x1, local copies, waits for them, and re-layouts  0.63 us

profile of v4, /device:TPU:0, one launch (start us, length us, event | category | flops | bytes accessed | tf_op | source)
XLA Modules:
  0.0 17.6 jit_solution(13832756659543131301)
XLA Ops:
  0.0 17.0 %shard_map.55 = f32[64,192]{1,0:T(8,128)S(1)} custom-call(s32[8]{0:T(128)} %sizes_in.1, s32[96]{0:T(128)} %home_in.1, s32[16]{0:T(128)} %row_irrep_in.1, f32[6,64,128]{2,1,0:T(8,128)} %amp.1, f32[192,16,128]{2,1,0:T(8,128)} %integ.1), custom_call_target="tpu_custom_call" | custom-call | tf_op jit(solution)/shard_map/pallas_call | solution.py:174
  17.0 0.6 %copy.7 = f32[64,192]{1,0:T(8,128)} copy(f32[64,192]{1,0:T(8,128)S(1)} %shard_map.55) | data formatting | bytes 98304
